TPU v7x, 512 devices: a whole 4x4x16 slice. The times are simulated.
512 devices in a mesh: scen: 16 (over x, y), comp: 32 (over z, core).
Axes of the slice: x: 4, y: 4, z: 16, core: 2. Of those that a mesh axis runs over, the one named last changes fastest.
Arguments:
- multiplier: float32 [256, 52, 16384], P('scen', None, 'comp'), may hold values from -2 to 2
- consensus_old: float32 [16, 52, 16384], P(None, None, 'comp'), may hold values from 0 to 1
- failure_week: int32 [256, 16384], P('scen', 'comp'), may hold values from 0 to 51
- crew_index: int32 [16384], P('comp'), may hold values from 0 to 255
- labor_hours: float32 [16384], P('comp'), may hold values from 0.5 to 1.5
- capacity: float32 [256, 52], replicated, may hold values from 6 to 25
- risk_weight: float32 [16384], P('comp'), may hold values from 0.5 to 2
- likelihood: float32 [256], P('scen'), may hold values from 0.1 to 1
- bundle_index: int32 [256], P('scen'), may hold values from 0 to 15, never falling along the last dimension, each value on 1 to 32 neighbouring positions
Outputs:
- multiplier_new: float32 [256, 52, 16384], P('scen', None, 'comp')
- bundle_consensus: float32 [256, 52, 16384], P('scen', None, 'comp')
Inputs may be any that keep to these rules, and one draw needn't show every extreme that they name: `bundle_index`: never falls along the scenarios; every bundle holds 1 to 32 scenarios, one exactly 32.
All inputs are finite; a program needn't handle non-finite values.
Results may differ from a plain program's by a relative error of at most 0.00013.
Values sent between devices are 32-bit elements; how exact they have to be, the bound alone decides.
A program may use at most 64 MiB of HBM per device.

v0:
```python
import jax
import jax.numpy as jnp
from jax import lax
from jax.sharding import PartitionSpec as P

ITERS = 3


step_size = 0.18
penalty = 1.0
crew_weight = 1.0


def target_plan(failure_week, week_count):
    week_index = jnp.arange(week_count, dtype=jnp.int32)[None, :, None]
    spacing = (failure_week[:, None, :] - week_index).astype(jnp.float32)
    return jnp.where(spacing >= 0, 1.0 / (1.0 + (spacing / 4.0) ** 2), 0.25)


def local(
    multiplier,
    consensus_old,
    failure_week,
    crew_index,
    labor_hours,
    capacity,
    risk_weight,
    likelihood,
    bundle_index,
):
    scen_rows, week_count, comp_cols = multiplier.shape
    bundle_count = consensus_old.shape[0]
    crew_count = capacity.shape[0]
    highest = lax.Precision.HIGHEST
    bundle_hot = (
        bundle_index[:, None] == jnp.arange(bundle_count, dtype=jnp.int32)[None, :]
    ).astype(jnp.float32)
    anchor = jnp.einsum("sb,bwc->swc", bundle_hot, consensus_old, precision=highest)
    target = target_plan(failure_week, week_count)
    crew_hot = (crew_index[:, None] == jnp.arange(crew_count, dtype=jnp.int32)[None, :]).astype(
        jnp.float32
    )
    labor_hot = crew_hot * labor_hours[:, None]
    coupling = crew_weight * crew_count / (comp_cols * lax.axis_size("comp"))
    limits = capacity.T[None, :, :]
    plan = anchor
    for sweep in range(ITERS):
        partial_load = jnp.einsum("swc,ck->swk", plan, labor_hot, precision=highest)
        crew_load = lax.psum(partial_load, "comp")
        excess = jnp.maximum(crew_load - limits, 0.0)
        pushed = jnp.einsum("swk,ck->swc", excess, crew_hot, precision=highest)
        slope = (
            risk_weight * (plan - target)
            + multiplier
            + penalty * (plan - anchor)
            + coupling * labor_hours * pushed
        )
        plan = jnp.clip(plan - step_size * slope, 0.0, 1.0)
    weighted = bundle_hot * likelihood[:, None]
    partial_totals = jnp.einsum("sb,swc->bwc", weighted, plan, precision=highest)
    partial_weights = jnp.sum(weighted, axis=0)
    totals, weight_sum = lax.psum((partial_totals, partial_weights), "scen")
    consensus = totals / weight_sum[:, None, None]
    bundle_consensus = jnp.einsum("sb,bwc->swc", bundle_hot, consensus, precision=highest)
    multiplier_new = multiplier + penalty * (plan - bundle_consensus)
    return (multiplier_new, bundle_consensus)


def solution(mesh):
    return jax.shard_map(
        local,
        mesh=mesh,
        in_specs=(
            P("scen", None, "comp"),
            P(None, None, "comp"),
            P("scen", "comp"),
            P("comp"),
            P("comp"),
            P(),
            P("comp"),
            P("scen"),
            P("scen"),
        ),
        out_specs=(P("scen", None, "comp"), P("scen", None, "comp")),
        check_vma=False,
    )
```

profile of v0, /device:TPU:1, one launch (start us, length us, event | category | flops | bytes accessed | tf_op | source)
XLA Modules:
  0.0 793.3 jit_solution(4020758842882281989)
XLA Ops:
  7.2 0.0 all-reduce.5.cloned.1.call-start
  7.2 1.4 copy-done
  8.6 1.6 fusion.37
  10.2 3.4 fusion.4
  13.7 0.0 all-reduce.5.cloned.1.call-update
  13.7 0.0 all-reduce.7.cloned.1.call-start
  13.8 211.6 %all-reduce.5.cloned.1.call-done = f32[16,52,256]{2,1,0:T(8,128)} async-done(((f32[16,52,256]{2,1,0:T(8,128)}), f32[16,52,256]{2,1,0:T(8,128)}) %all-reduce.5.cloned.1.call-update) | async-done | bytes 851984 | tf_op jit(solution)/shard_map/psum | solution.py:49
  225.3 1.4 subtract_maximum_fusion.2
  226.7 0.3 copy-done.7
  227.0 2.0 subtract_clamp_fusion.2
  229.1 1.2 copy-done.5
  230.2 3.5 fusion.2
  233.7 0.0 all-reduce.7.cloned.1.call-update
  233.7 0.2 all-reduce.9.cloned.1.call-start
  233.9 205.5 %all-reduce.7.cloned.1.call-done = f32[16,52,256]{2,1,0:T(8,128)} async-done(((f32[16,52,256]{2,1,0:T(8,128)}), f32[16,52,256]{2,1,0:T(8,128)}) %all-reduce.7.cloned.1.call-update) | async-done | bytes 851984 | tf_op jit(solution)/shard_map/psum | solution.py:49
  439.4 1.4 subtract_maximum_fusion.1
  440.8 0.4 copy-done.6
  441.2 3.5 subtract_clamp_fusion.1
  444.7 1.2 copy-done.3
  445.8 3.5 fusion
  449.3 0.0 all-reduce.9.cloned.1.call-update
  449.3 0.0 all-reduce.11.cloned.1.call-start
  449.4 205.7 %all-reduce.9.cloned.1.call-done = f32[16,52,256]{2,1,0:T(8,128)} async-done(((f32[16,52,256]{2,1,0:T(8,128)}), f32[16,52,256]{2,1,0:T(8,128)}) %all-reduce.9.cloned.1.call-update) | async-done | bytes 851984 | tf_op jit(solution)/shard_map/psum | solution.py:49
  655.1 1.4 subtract_maximum_fusion
  656.4 0.4 copy-done.4
  656.8 3.5 subtract_clamp_fusion
  660.3 1.2 copy-done.1
  661.5 2.8 fusion.34
  664.4 0.1 select_reduce_fusion
  664.4 33.5 %psum.39 = f32[16]{0:T(128)S(1)} all-reduce(f32[16]{0:T(128)S(1)} %select_reduce_fusion), channel_id=1, replica_groups=mesh['scen'=16,'comp'=32] {'scen'}, use_global_device_ids=true, to_apply=%region_5.6 | all-reduce | flops 16 | bytes 128 | tf_op jit(solution)/shard_map/psum | solution.py:62
  697.9 84.0 %all-reduce.11.cloned.1.call-done = f32[16,52,512]{2,0,1:T(8,128)} async-done(((f32[16,52,512]{2,0,1:T(8,128)}), f32[16,52,512]{2,0,1:T(8,128)}) %all-reduce.11.cloned.1.call-update) | async-done | bytes 1703952 | tf_op jit(solution)/shard_map/psum | solution.py:62
  781.9 4.9 subtract_add_fusion
  (25 shorter events, 0.1 us)
Async XLA Ops:
  7.2 1.5 copy-start
  7.2 3.0 copy-start.10
  7.2 3.0 copy-start.9
  7.2 218.1 %all-reduce.5.cloned.1.call-start = ((), (), s32[]{:S(2)}) async-start(), calls=%async_computation | async-start | bytes 1835008 | tf_op jit(solution)/shard_map/psum | solution.py:49
  10.2 215.1 %copy-start.8 = (f32[256,52]{0,1:T(8,128)S(1)}, f32[256,52]{0,1:T(8,128)}, u32[]{:S(2)}) copy-start(f32[256,52]{0,1:T(8,128)} %param.14) | copy-start | bytes 159748
  13.7 213.0 %copy-start.13 = (s32[16,512]{1,0:T(8,128)S(1)}, s32[16,512]{1,0:T(8,128)}, u32[]{:S(2)}) copy-start(s32[16,512]{1,0:T(8,128)} %param.11) | copy-start | bytes 98308
  13.7 213.0 %copy-start.14 = (f32[512]{0:T(512)S(1)}, f32[512]{0:T(512)}, u32[]{:S(2)}) copy-start(f32[512]{0:T(512)} %param.15) | copy-start | bytes 6148
  13.7 425.7 %all-reduce.7.cloned.1.call-start = ((), (), s32[]{:S(2)}) async-start(), calls=%async_computation.1 | async-start | bytes 1835008 | tf_op jit(solution)/shard_map/psum | solution.py:49
  225.3 1.7 copy-start.7
  229.0 1.2 copy-start.5
  233.7 421.3 %all-reduce.9.cloned.1.call-start = ((), (), s32[]{:S(2)}) async-start(), calls=%async_computation.2 | async-start | bytes 1835008 | tf_op jit(solution)/shard_map/psum | solution.py:49
  439.4 1.7 copy-start.6
  444.6 1.2 copy-start.3
  449.3 332.6 %all-reduce.11.cloned.1.call-start = ((), (), s32[]{:S(2)}) async-start(), calls=%async_computation.3 | async-start | bytes 3407872 | tf_op jit(solution)/shard_map/psum | solution.py:62
  655.1 1.7 copy-start.4
  656.8 4.7 copy-start.11
  656.8 4.7 copy-start.12
  660.3 1.2 copy-start.1
  664.3 117.6 %copy-start.2 = (f32[16,52,512]{2,0,1:T(8,128)S(1)}, f32[16,52,512]{2,0,1:T(8,128)}, u32[]{:S(2)}) copy-start(f32[16,52,512]{2,0,1:T(8,128)} %copy-done.1) | copy-start | bytes 5111812
Sparse Core Ops, SparseCore 0:
  13.8 211.4 all-reduce.4
  233.8 205.5 all-reduce.6
  449.4 205.5 all-reduce.8
  664.5 117.3 all-reduce.10
where the time goes:
time: 794 us; the launch traced here: 793 us
  waiting for transfers between devices  707 us (89%)
  blocking collectives  33.5 us (4%)
  matrix products  28.6 us (4%)
  between operations  13.9 us (2%)
    psum x3, waiting for transfers between devices, local(): crew_load = lax.psum(partial_load, 'comp')  623 us
    psum x1, waiting for transfers between devices, local(): totals, weight_sum = lax.psum((partial_totals, partial_weights), 'scen')  84 us
    psum x1, blocking collectives, local(): totals, weight_sum = lax.psum((partial_totals, partial_weights), 'scen')  33.5 us
  transfers between devices with their start and end apart: 4, of which 4 were waited for; matrix products, arithmetic and copies ran while one was open for 0% of the time, Pallas kernels for 0%

commit v1 on v0

v1 whole, which is shorter than its diff:
```python
import jax
import jax.numpy as jnp
from jax import lax
from jax.experimental import pallas as pl
from jax.experimental.pallas import tpu as pltpu
from jax.sharding import PartitionSpec as P

MESH = pl.DeviceIdType.MESH
ITERS = 3
STEP = 0.18
CREW_WEIGHT = 1.0
PLACES = (6, -6, 3, -3, 0, 7, -5, 4, -2, 1, 5, -7, 2, -4, -1, 8)
GROUPS = ((0, 24), (24, 32))
NCOPY = 17


def split(x):
    high = x.astype(jnp.bfloat16)
    low = (x - high.astype(jnp.float32)).astype(jnp.bfloat16)
    return high, low


def kernel(
    mult_hbm, cons_hbm, fw_ref, crew_ref, labor_ref, cap_ref, risk_ref, like_ref, bundle_ref,
    new_ref, bc_ref,
    mult, cons, plan, base, hot, cap_t, cap_pad, runs, sums,
    part0, part1, core0, core1, near0, near1, opp0, opp1, hub0, hub1, far0, far1, exc0, exc1,
    edge0, edge1, got0, got1,
    load_sem, send_sem, recv_sem, edge_send, edge_recv,
):
    scen_count = lax.axis_size("scen")
    comp_count = lax.axis_size("comp")
    chips = comp_count // 2
    me_s = lax.axis_index("scen")
    me_c = lax.axis_index("comp")
    z = me_c // 2
    k = lax.rem(me_c, 2)
    rows_s, weeks, cols = mult.shape
    crews = hot.shape[0]
    half = crews // 2
    parts, cores, nears, opps = (part0, part1), (core0, core1), (near0, near1), (opp0, opp1)
    hubs, fars, excs = (hub0, hub1), (far0, far1), (exc0, exc1)
    edges, gots = (edge0, edge1), (got0, got1)

    def chip(step):
        return (me_s, lax.rem(z + step + chips, chips) * 2 + k)

    def row(step):
        return (lax.rem(me_s + step + scen_count, scen_count), me_c)

    other = (me_s, z * 2 + 1 - k)

    cons_in = pltpu.make_async_copy(cons_hbm, cons, load_sem.at[0])
    mult_in = pltpu.make_async_copy(mult_hbm, mult, load_sem.at[1])
    cons_in.start()
    mult_in.start()

    barrier = pltpu.get_barrier_semaphore()
    greeted = [other] + [chip(n) for n in (1, -1, 2, -2, 3, -3, 6, -6)] + [row(1), row(-1)]
    for device in greeted:
        pl.semaphore_signal(barrier, inc=1, device_id=device, device_id_type=MESH)

    hot[...] = (
        lax.broadcasted_iota(jnp.int32, (crews, cols), 0) == crew_ref[...]
    ).astype(jnp.bfloat16)
    cap_pad[...] = jnp.zeros_like(cap_pad)
    cap_pad[:, :weeks] = cap_ref[pl.ds(pl.multiple_of(k * half, half), half), :]
    cap_t[...] = cap_pad[...].T
    plan[...] = jnp.zeros_like(plan)
    base[...] = jnp.zeros_like(base)
    labor = labor_ref[...]
    risk = risk_ref[...]
    coupling = CREW_WEIGHT * crews / (cols * comp_count)
    alpha = 1.0 - STEP * (risk + 1.0)
    beta = (STEP * coupling) * labor

    def scenario(place):
        return lax.rem(z + PLACES[place] + chips, chips)

    def load(g, place, x):
        rows = GROUPS[g][1]
        high, low = split(x * labor)
        dims = (((1,), (1,)), ((), ()))
        out = lax.dot_general(high, hot[...], dims, preferred_element_type=jnp.float32)
        out = out + lax.dot_general(low, hot[...], dims, preferred_element_type=jnp.float32)
        count = x.shape[0] // rows
        for h in range(2):
            parts[g][h, pl.ds(place, count)] = out[:, h * half:(h + 1) * half].reshape(
                count, rows, half
            )

    def copy(g, t, n, source, target, device):
        at = (g * ITERS + t) * NCOPY + n
        return pltpu.make_async_remote_copy(
            src_ref=source, dst_ref=target, send_sem=send_sem.at[at], recv_sem=recv_sem.at[at],
            device_id=device, device_id_type=MESH,
        )

    flying = {}

    def sent(g, t, numbers):
        for n in numbers:
            flying.pop((g, t, n)).wait_send()

    def arrive(g, t, numbers):
        for n in numbers:
            flying[g, t, n].wait_recv()

    def start(g, t, n, source, target, device):
        c = copy(g, t, n, source, target, device)
        c.start()
        flying[g, t, n] = c

    def update(g, t):
        first, rows = GROUPS[g]
        for place in range(0, rows_s, 4):
            scens = pl.ds(place, 4)
            weeks_at = pl.ds(first, rows)
            old = plan[scens, weeks_at, :].reshape(4 * rows, cols)
            if t >= 0:
                pushed = 0.0
                for h in range(2):
                    high, low = split(excs[g][t, h, scens].reshape(4 * rows, half))
                    way = hot[h * half:(h + 1) * half, :]
                    pushed = pushed + jnp.dot(high, way, preferred_element_type=jnp.float32)
                    pushed = pushed + jnp.dot(low, way, preferred_element_type=jnp.float32)
                old = jnp.clip(
                    alpha * old + base[scens, weeks_at, :].reshape(4 * rows, cols) - beta * pushed,
                    0.0, 1.0,
                )
                if t < ITERS - 1:
                    plan[scens, weeks_at, :] = old.reshape(4, rows, cols)
                else:
                    for n in range(4):
                        runs[scenario(place + n), weeks_at, :] = old[n * rows:(n + 1) * rows]
            if t < ITERS - 1:
                load(g, place, old)

    def phase_core(g, t):
        if t > 0:
            sent(g, t - 1, (0,))
        update(g, t - 1)
        if t == 0 and g == 0:
            pl.semaphore_wait(barrier, len(greeted))
        start(g, t, 0, parts[g].at[1 - k], cores[g].at[t], other)

    def phase_near(g, t):
        arrive(g, t, (0,))
        cores[g][t] = cores[g][t] + parts[g][k]
        mine = cores[g].at[t]
        start(g, t, 1, mine.at[pl.ds(5, 5)], nears[g].at[t, 0], chip(1))
        start(g, t, 2, mine.at[pl.ds(10, 5)], nears[g].at[t, 1], chip(-1))
        start(g, t, 3, mine.at[15], opps[g].at[t], chip(4 * k - 2))

    def phase_far(g, t):
        if t > 0:
            sent(g, t - 1, (4, 5, 6, 7))
        arrive(g, t, (1, 2, 3))
        hubs[g][...] = cores[g][t, 0:5] + nears[g][t, 0] + nears[g][t, 1]
        hubs[g][1 - k] = hubs[g][1 - k] + opps[g][t]
        for n, step in enumerate((6, -6, 3, -3)):
            start(g, t, 4 + n, hubs[g].at[n], fars[g].at[t, n], chip(step))

    def phase_back(g, t):
        arrive(g, t, range(4, 8))
        far = fars[g][t]
        total = hubs[g][4] + (far[0] + far[1]) + (far[2] + far[3])
        first, rows = GROUPS[g]
        excs[g][t, k, 4] = jnp.maximum(total - cap_t[first:first + rows, :], 0.0)
        own = excs[g].at[t, k, 4]
        for n, step in enumerate((6, -6, 3, -3)):
            start(g, t, 8 + n, own, excs[g].at[t, k, n ^ 1], chip(step))

    def phase_spread(g, t):
        arrive(g, t, range(8, 12))
        mine = excs[g].at[t, k]
        start(g, t, 12, mine.at[pl.ds(0, 5)], mine.at[pl.ds(10, 5)], chip(1))
        start(g, t, 13, mine.at[pl.ds(0, 5)], mine.at[pl.ds(5, 5)], chip(-1))
        start(g, t, 14, mine.at[1 - k], mine.at[15], chip(2 - 4 * k))
        start(g, t, 15, mine.at[pl.ds(0, 5)], mine.at[pl.ds(0, 5)], other)

    def phase_share(g, t):
        arrive(g, t, (12, 13, 14))
        mine = excs[g].at[t, k]
        start(g, t, 16, mine.at[pl.ds(5, 11)], mine.at[pl.ds(5, 11)], other)

    def phase_end(g, t):
        arrive(g, t, (15, 16))

    cons_in.wait()
    for place in range(rows_s):
        plan[place, :weeks, :] = cons[bundle_ref[scenario(place)]]
    groups = range(len(GROUPS))
    for t in range(ITERS):
        for g in groups:
            if t > 0:
                phase_end(g, t - 1)
            phase_core(g, t)
        for g in groups:
            phase_near(g, t)
        if t == 0:
            mult_in.wait()
            week = lax.broadcasted_iota(jnp.int32, (weeks, cols), 0)
            for place in range(rows_s):
                d = scenario(place)
                spacing = (fw_ref[pl.ds(d, 1), :] - week).astype(jnp.float32)
                target = jnp.where(spacing >= 0, 1.0 / (1.0 + (spacing * 0.25) ** 2), 0.25)
                base[place, :weeks, :] = STEP * (
                    risk * target - mult[d] + plan[place, :weeks, :]
                )
        for phase in (phase_far, phase_back, phase_spread, phase_share):
            for g in groups:
                phase(g, t)

    last = rows_s - 1
    head, tail = bundle_ref[0], bundle_ref[last]
    moving = {}

    def edge_start(g, n, source, step):
        at = g * 4 + n
        moving[g, n] = pltpu.make_async_remote_copy(
            src_ref=source, dst_ref=gots[g].at[n], send_sem=edge_send.at[at],
            recv_sem=edge_recv.at[at], device_id=row(step), device_id_type=MESH,
        )
        moving[g, n].start()

    for g in groups:
        first, rows = GROUPS[g]
        phase_end(g, ITERS - 1)
        update(g, ITERS - 1)
        for n, (which, step) in enumerate(((tail, 1), (head, -1))):

            def body(s, carry):
                total, weight = carry
                factor = jnp.where(bundle_ref[s] == which, like_ref[s], 0.0)
                return total + factor * runs[s, first:first + rows, :], weight + factor

            total, weight = lax.fori_loop(
                0, rows_s, body, (jnp.zeros((rows, cols), jnp.float32), jnp.float32(0.0))
            )
            edges[g][n, 0:rows] = total
            edges[g][n, rows:rows + 8] = jnp.where(
                lax.broadcasted_iota(jnp.int32, (8, cols), 0) < 4,
                which.astype(jnp.float32), weight,
            )
            edge_start(g, n, edges[g].at[n], step)
    for g in groups:
        for n, step in enumerate((1, -1)):
            moving[g, n].wait_recv()
            edge_start(g, n + 2, gots[g].at[n], step)
    for g in groups:
        first, rows = GROUPS[g]
        live = min(weeks - first, rows)
        got = gots[g]
        for n in (2, 3):
            moving[g, n].wait_recv()

        def arrived(n, which):
            same = got[n, rows:rows + 1, :] == which.astype(jnp.float32)
            return (
                jnp.where(same, got[n, 0:rows], 0.0),
                jnp.where(same, got[n, rows + 4:rows + 5, :], 0.0),
            )

        def both(n, which):
            one, two = arrived(n, which), arrived(n + 2, which)
            return one[0] + two[0], one[1] + two[1]

        total, weight = both(0, head)
        for s in range(rows_s):
            if s:
                keep = jnp.where(bundle_ref[s] == bundle_ref[s - 1], 1.0, 0.0)
                total, weight = total * keep, weight * keep
            total = total + like_ref[s] * runs[s, first:first + rows, :]
            weight = weight + like_ref[s]
            if s < last:
                sums[s, 0:rows] = total
                sums[s, rows:rows + 1] = weight
        add = both(1, tail)
        mean = (total + add[0]) / (weight + add[1])
        for s in range(last, -1, -1):
            if s < last:
                mean = jnp.where(
                    bundle_ref[s] == bundle_ref[s + 1],
                    mean, sums[s, 0:rows] / sums[s, rows:rows + 1],
                )
            weeks_at = slice(first, first + live)
            bc_ref[s, weeks_at, :] = mean[:live]
            new_ref[s, weeks_at, :] = (
                mult[s, weeks_at, :] + (runs[s, weeks_at, :] - mean[:live])
            )
    for c in (*flying.values(), *moving.values()):
        c.wait_send()


def local(
    multiplier, consensus_old, failure_week, crew_index, labor_hours, capacity, risk_weight,
    likelihood, bundle_index,
):
    rows_s, weeks, cols = multiplier.shape
    crews = capacity.shape[0]
    half = crews // 2
    padded = sum(rows for _, rows in GROUPS)
    f32 = jnp.float32

    def each(*shape):
        return [
            pltpu.VMEM(tuple(rows + 8 if n == "e" else rows if n == "r" else n for n in shape), f32)
            for _, rows in GROUPS
        ]

    vmem, smem, anywhere = (
        pl.BlockSpec(memory_space=m) for m in (pltpu.VMEM, pltpu.SMEM, pl.ANY)
    )
    copies = len(GROUPS) * ITERS * NCOPY
    return pl.pallas_call(
        kernel,
        out_shape=[jax.ShapeDtypeStruct(multiplier.shape, f32)] * 2,
        in_specs=[anywhere, anywhere, vmem, vmem, vmem, vmem, vmem, smem, smem],
        out_specs=[vmem, vmem],
        scratch_shapes=[
            pltpu.VMEM((rows_s, weeks, cols), f32),
            pltpu.VMEM((rows_s, weeks, cols), f32),
            pltpu.VMEM((rows_s, padded, cols), f32),
            pltpu.VMEM((rows_s, padded, cols), f32),
            pltpu.VMEM((crews, cols), jnp.bfloat16),
            pltpu.VMEM((half, 128), f32),
            pltpu.VMEM((128, half), f32),
            pltpu.VMEM((rows_s, padded, cols), f32),
            pltpu.VMEM((rows_s, max(rows for _, rows in GROUPS) + 8, cols), f32),
            *each(2, rows_s, "r", half),
            *each(ITERS, rows_s, "r", half),
            *each(ITERS, 2, 5, "r", half),
            *each(ITERS, "r", half),
            *each(5, "r", half),
            *each(ITERS, 4, "r", half),
            *each(ITERS, 2, rows_s, "r", half),
            *each(2, "e", cols),
            *each(4, "e", cols),
            pltpu.SemaphoreType.DMA((2,)),
            pltpu.SemaphoreType.DMA((copies,)),
            pltpu.SemaphoreType.DMA((copies,)),
            pltpu.SemaphoreType.DMA((4 * len(GROUPS),)),
            pltpu.SemaphoreType.DMA((4 * len(GROUPS),)),
        ],
        compiler_params=pltpu.CompilerParams(
            collective_id=0, has_side_effects=True, vmem_limit_bytes=48 << 20
        ),
        name="hedge",
    )(
        multiplier, consensus_old, failure_week, crew_index.reshape(1, -1),
        labor_hours.reshape(1, -1), capacity, risk_weight.reshape(1, -1), likelihood, bundle_index,
    )


def solution(mesh):
    return jax.shard_map(
        local,
        mesh=mesh,
        in_specs=(
            P("scen", None, "comp"),
            P(None, None, "comp"),
            P("scen", "comp"),
            P("comp"),
            P("comp"),
            P(),
            P("comp"),
            P("scen"),
            P("scen"),
        ),
        out_specs=(P("scen", None, "comp"), P("scen", None, "comp")),
        check_vma=False,
    )
```

time: 794 us -> 126 us (0.16)
  waiting for transfers between devices: 707 us -> 0 us
  Pallas kernels: 0 us -> 115 us
  blocking collectives: 33.5 us -> 0 us
  matrix products: 28.6 us -> 0 us
  between operations: 13.9 us -> 0.73 us
    psum x4 -> x0, waiting for transfers between devices: 707 us -> none  [the longest x3 623 us: local(): crew_load = lax.psum(partial_load, 'comp')]
    pallas_call x0 -> x1, Pallas kernels: none -> 115 us  [local(): pl.pallas_call(kernel, out_shape=[jax.ShapeDtypeStruct(multiplier.shape,...]
    psum x1 -> x0, blocking collectives: 33.5 us -> none  [local(): totals, weight_sum = lax.psum((partial_totals, partial_weights), 'scen')]
    dot_general x9 -> x0, matrix products: 28.6 us -> none  [the longest x3 10.3 us: local(): partial_load = jnp.einsum('swc,ck->swk', plan, labor_hot, precision=highest)]
  transfers between devices with their start and end apart: 4 -> 0, of which waited for: 4 -> 0; matrix products, arithmetic and copies ran while one was open for 0% -> 0% of each run, Pallas kernels for 0% -> 0%
where the time goes in v1:
time: 126 us
  Pallas kernels  115 us (91%)
  local copies, waits for them, and re-layouts  10.1 us (8%)
    pallas_call x1, Pallas kernels, local(): pl.pallas_call(kernel, out_shape=[jax.ShapeDtypeStruct(multiplier.shape,...  115 us
    unnamed x17, local copies, waits for them, and re-layouts  5.77 us
    pallas_call x2, local copies, waits for them, and re-layouts, local(): pl.pallas_call(kernel, out_shape=[jax.ShapeDtypeStruct(multiplier.shape,...  4.35 us

profile of v1, /device:TPU:1, one launch (start us, length us, event | category | flops | bytes accessed | tf_op | source)
XLA Modules:
  0.0 126.2 jit_solution(11503181980618307152)
XLA Ops:
  0.6 0.0 copy-start.6
  0.6 1.0 copy.13.cap_ref
  1.7 2.4 %copy.11.mult_hbm = f32[16,52,512]{2,1,0:T(8,128)S(1)} copy(f32[16,52,512]{2,0,1:T(8,128)} %param.9) | data formatting | bytes 3407872 | tf_op args[0]
  4.1 0.0 copy-done.6
  4.1 0.0 copy-start
  4.2 0.0 copy-start.1
  4.2 0.0 copy-start.2
  4.2 0.0 copy-start.3
  4.2 0.0 copy-start.4
  4.2 0.0 copy-start.5
  4.2 2.2 %copy.12.cons_hbm = f32[16,52,512]{2,1,0:T(8,128)} copy(f32[16,52,512]{2,0,1:T(8,128)S(1)} %copy-done.6) | data formatting | bytes 3407872 | tf_op args[1]
  6.5 0.0 copy-done
  6.5 0.0 copy-done.1
  6.5 0.0 copy-done.2
  6.5 0.0 copy-done.3
  6.5 0.0 copy-done.4
  6.5 0.0 copy-done.5
  6.5 115.4 %hedge.1 = (f32[16,52,512]{2,1,0:T(8,128)S(1)}, f32[16,52,512]{2,1,0:T(8,128)S(1)}) custom-call(f32[16,52,512]{2,1,0:T(8,128)S(1)} %copy.11.mult_hbm, f32[16,52,512]{2,1,0:T(8,128)} %copy.12.cons_hbm, s32[16,512]{1,0:T(8,128)S(1)} %copy-done, s32[1,512]{1,0:T(1,128)S(1)} %bitcast.3, f32[1,512]{1,0:T(1,128)S(1)} %bitcast.4, f32[256,52]{1,0:T(8,128)S(1)} %copy.13.cap_ref, ...), custom_call_target="tpu_custom_call" | custom-call | tf_op jit(solution)/shard_map/hedge/pallas_call | solution.py:316
  121.9 2.2 %copy.14 = f32[16,52,512]{2,0,1:T(8,128)} copy(f32[16,52,512]{2,1,0:T(8,128)S(1)} %get-tuple-element.2) | data formatting | bytes 3407872 | tf_op jit(solution)/shard_map/hedge/pallas_call | solution.py:316
  124.0 2.2 %copy.15 = f32[16,52,512]{2,0,1:T(8,128)} copy(f32[16,52,512]{2,1,0:T(8,128)S(1)} %get-tuple-element.3) | data formatting | bytes 3407872 | tf_op jit(solution)/shard_map/hedge/pallas_call | solution.py:316
Async XLA Ops:
  0.6 3.5 %copy-start.6 = (f32[16,52,512]{2,0,1:T(8,128)S(1)}, f32[16,52,512]{2,0,1:T(8,128)}, u32[]{:S(2)}) copy-start(f32[16,52,512]{2,0,1:T(8,128)} %param.10) | copy-start | bytes 5111812
  4.1 2.3 %copy-start = (s32[16,512]{1,0:T(8,128)S(1)}, s32[16,512]{1,0:T(8,128)}, u32[]{:S(2)}) copy-start(s32[16,512]{1,0:T(8,128)} %fw_ref.1) | copy-start | bytes 98308
  4.2 2.3 %copy-start.1 = (s32[512]{0:T(512)S(1)}, s32[512]{0:T(512)}, u32[]{:S(2)}) copy-start(s32[512]{0:T(512)} %param.12) | copy-start | bytes 6148
  4.2 2.3 %copy-start.2 = (f32[512]{0:T(512)S(1)}, f32[512]{0:T(512)}, u32[]{:S(2)}) copy-start(f32[512]{0:T(512)} %param.13) | copy-start | bytes 6148
  4.2 2.3 %copy-start.3 = (f32[512]{0:T(512)S(1)}, f32[512]{0:T(512)}, u32[]{:S(2)}) copy-start(f32[512]{0:T(512)} %param.15) | copy-start | bytes 6148
  4.2 2.3 %copy-start.4 = (f32[16]{0:T(128)S(1)}, f32[16]{0:T(128)}, u32[]{:S(2)}) copy-start(f32[16]{0:T(128)} %like_ref.1) | copy-start | bytes 196
  4.2 2.3 %copy-start.5 = (s32[16]{0:T(128)S(1)}, s32[16]{0:T(128)}, u32[]{:S(2)}) copy-start(s32[16]{0:T(128)} %bundle_ref.1) | copy-start | bytes 196

commit v2 on v0

v2 whole, which is shorter than its diff:
```python
import jax
import jax.numpy as jnp
from jax import lax
from jax.experimental import pallas as pl
from jax.experimental.pallas import tpu as pltpu
from jax.sharding import PartitionSpec as P

MESH = pl.DeviceIdType.MESH
ITERS = 3
STEP = 0.18
CREW_WEIGHT = 1.0
PLACES = (6, -6, 3, -3, 0, 7, -5, 4, -2, 1, 5, -7, 2, -4, -1, 8)
TILES = (2, 2, 2, 1)
ORDER = (
    0, 1, 2, 3, 0, 1, 2, 3, 0, 1, 2, 3, 0, 1, 2, 3, 0, 1, 2, 3,
    0, 1, 0, 2, 1, 3, 0, 2, 1, 3, 2, 3, 0, 1, 2, 3, 0, 1, 2, 3,
    0, 1, 2, 3, 0, 1, 0, 2, 1, 3, 0, 2, 1, 3, 2, 3, 0, 1, 2, 3,
    0, 1, 2, 3, 0, 1, 2, 3, 0, 1, 0, 2, 1, 3, 2, 3,
)
NCOPY = 17
F32, BF16 = jnp.float32, jnp.bfloat16


def split(x):
    high = x.astype(BF16)
    low = (x - high.astype(F32)).astype(BF16)
    return high, low


def dot(a, b):
    return jnp.dot(a, b, preferred_element_type=F32)


def kernel(
    mult_hbm, cons_hbm, fw_hbm, crew_hbm, labor_hbm, cap_hbm, risk_hbm, like_hbm, bundle_hbm,
    new_ref, bc_ref,
    fw_ref, crew_ref, labor_ref, cap_ref, risk_ref, like_ref, bundle_ref,
    mult, cons, plan, base, hot, cap_rows, mixer, likes, means,
    load_sem, store_sem, send_sem, recv_sem,
    edge_send, edge_recv, *per_group,
):
    groups = range(len(TILES))
    parts, cores, nears, opps, hubs, fars, excs, edges, gots = (
        per_group[n:n + len(TILES)] for n in range(0, len(per_group), len(TILES))
    )
    scen_count = lax.axis_size("scen")
    comp_count = lax.axis_size("comp")
    chips = comp_count // 2
    me_s = lax.axis_index("scen")
    me_c = lax.axis_index("comp")
    z = me_c // 2
    k = lax.rem(me_c, 2)
    weeks = cap_ref.shape[0]
    live, cols = mult_hbm.shape
    scens = live // weeks
    crews = hot.shape[0]
    half = crews // 2
    rows_of = [8 * n for n in TILES]
    first_of = [chips * sum(rows_of[:g]) for g in groups]

    def chip(step):
        return (me_s, lax.rem(z + step + chips, chips) * 2 + k)

    def row(step):
        return (lax.rem(me_s + step + scen_count, scen_count), me_c)

    def block(g, step):
        d = lax.rem(z + step + chips, chips)
        return pl.ds(pl.multiple_of(first_of[g] + d * rows_of[g], 8), rows_of[g])

    other = (me_s, z * 2 + 1 - k)

    loads = [
        pltpu.make_async_copy(source, target, load_sem.at[n])
        for n, (source, target) in enumerate((
            (crew_hbm, crew_ref), (bundle_hbm, bundle_ref), (labor_hbm, labor_ref),
            (cons_hbm, cons), (risk_hbm, risk_ref), (cap_hbm, cap_ref), (like_hbm, like_ref),
            (fw_hbm, fw_ref), (mult_hbm, mult),
        ))
    ]
    for load in loads:
        load.start()

    barrier = pltpu.get_barrier_semaphore()
    greeted = [other] + [chip(n) for n in (1, -1, 2, -2, 3, -3, 6, -6)] + [row(n) for n in (1, -1, 2, -2)]
    for device in greeted:
        pl.semaphore_signal(barrier, inc=1, device_id=device, device_id_type=MESH)

    padded = plan.shape[0]
    plan[live:, :] = jnp.zeros((padded - live, cols), F32)
    base[live:, :] = jnp.zeros((padded - live, cols), F32)
    cap_rows[live:, :] = jnp.zeros((padded - live, half), F32)
    loads[0].wait()
    hot[...] = (
        lax.broadcasted_iota(jnp.int32, (crews, cols), 0) == crew_ref[...]
    ).astype(BF16)
    coupling = CREW_WEIGHT * crews / (cols * comp_count)

    def by_scenario(ref, scenario):
        out = jnp.full(scenario.shape, ref[0])
        for s in range(1, scens):
            out = jnp.where(scenario == s, ref[s], out)
        return out

    loads[1].wait()
    span = 256
    r = lax.broadcasted_iota(jnp.int32, (span, span), 0)
    c = lax.broadcasted_iota(jnp.int32, (span, span), 1)
    want = by_scenario(bundle_ref, lax.rem(lax.broadcasted_iota(jnp.int32, (span, 128), 0), scens))
    want = jnp.concatenate([want] * (span // 128), axis=1)
    mixer[...] = (want + (r // scens) * scens == c).astype(BF16)
    loads[3].wait()
    loads[2].wait()
    labor = labor_ref[...]
    for at in range(0, live, span):
        size = min(span, live - at)
        x = cons[at:at + size, :]
        high, low = split(x)
        lower = (x - high.astype(F32) - low.astype(F32)).astype(BF16)
        take = mixer[:size, :size]
        plan[at:at + size, :] = dot(take, high) + dot(take, low) + dot(take, lower)

    flying = {}

    def start(g, t, n, source, target, device):
        at = (g * ITERS + t) * NCOPY + n
        flying[g, t, n] = pltpu.make_async_remote_copy(
            src_ref=source, dst_ref=target, send_sem=send_sem.at[at], recv_sem=recv_sem.at[at],
            device_id=device, device_id_type=MESH,
        )
        flying[g, t, n].start()

    def sent(g, t, numbers):
        for n in numbers:
            flying.pop((g, t, n)).wait_send()

    def arrive(g, t, numbers):
        for n in numbers:
            flying[g, t, n].wait_recv()

    def update(g, t):
        rows = rows_of[g]
        many = chips if TILES[g] == 1 else 8 if TILES[g] == 2 else 4
        for place in range(0, chips, many):
            blocks = [block(g, PLACES[place + n]) for n in range(many)]
            old = jnp.concatenate([plan[b, :] for b in blocks], axis=0)
            if t >= 0:
                fixed = jnp.concatenate([base[b, :] for b in blocks], axis=0)
                pushed = 0.0
                for h in range(2):
                    high, low = split(
                        excs[g][t, h, place:place + many].reshape(many * rows, half)
                    )
                    way = hot[h * half:(h + 1) * half, :]
                    pushed = pushed + dot(high, way) + dot(low, way)
                alpha = 1.0 - STEP * (risk_ref[...] + 1.0)
                beta = (STEP * coupling) * labor
                old = jnp.clip(alpha * old + fixed - beta * pushed, 0.0, 1.0)
                for n, b in enumerate(blocks):
                    plan[b, :] = old[n * rows:(n + 1) * rows]
            if t < ITERS - 1:
                high, low = split(old * labor)
                dims = (((1,), (1,)), ((), ()))
                out = lax.dot_general(high, hot[...], dims, preferred_element_type=F32)
                out = out + lax.dot_general(low, hot[...], dims, preferred_element_type=F32)
                for h in range(2):
                    parts[g][h, place:place + many] = out[:, h * half:(h + 1) * half].reshape(
                        many, rows, half
                    )

    def phase_core(g, t):
        if t > 0:
            arrive(g, t - 1, (15, 16))
            sent(g, t - 1, (0,))
        update(g, t - 1)
        if t == 0 and g == 0:
            pl.semaphore_wait(barrier, len(greeted))
        start(g, t, 0, parts[g].at[1 - k], cores[g].at[t], other)

    def phase_near(g, t):
        arrive(g, t, (0,))
        cores[g][t] = cores[g][t] + parts[g][k]
        mine = cores[g].at[t]
        start(g, t, 1, mine.at[pl.ds(5, 5)], nears[g].at[t, 0], chip(1))
        start(g, t, 2, mine.at[pl.ds(10, 5)], nears[g].at[t, 1], chip(-1))
        start(g, t, 3, mine.at[15], opps[g].at[t], chip(4 * k - 2))

    def phase_far(g, t):
        if t > 0:
            sent(g, t - 1, (4, 5, 6, 7))
        arrive(g, t, (1, 2, 3))
        hubs[g][...] = cores[g][t, 0:5] + nears[g][t, 0] + nears[g][t, 1]
        hubs[g][1 - k] = hubs[g][1 - k] + opps[g][t]
        for n, step in enumerate((6, -6, 3, -3)):
            start(g, t, 4 + n, hubs[g].at[n], fars[g].at[t, n], chip(step))

    def phase_back(g, t):
        arrive(g, t, range(4, 8))
        far = fars[g][t]
        total = hubs[g][4] + (far[0] + far[1]) + (far[2] + far[3])
        excs[g][t, k, 4] = jnp.maximum(total - cap_rows[block(g, 0), :], 0.0)
        own = excs[g].at[t, k, 4]
        for n, step in enumerate((6, -6, 3, -3)):
            start(g, t, 8 + n, own, excs[g].at[t, k, n ^ 1], chip(step))

    def phase_spread(g, t):
        arrive(g, t, range(8, 12))
        mine = excs[g].at[t, k]
        start(g, t, 12, mine.at[pl.ds(0, 5)], mine.at[pl.ds(10, 5)], chip(1))
        start(g, t, 13, mine.at[pl.ds(0, 5)], mine.at[pl.ds(5, 5)], chip(-1))
        start(g, t, 14, mine.at[1 - k], mine.at[15], chip(2 - 4 * k))
        start(g, t, 15, mine.at[pl.ds(0, 5)], mine.at[pl.ds(0, 5)], other)

    def phase_share(g, t):
        arrive(g, t, (12, 13, 14))
        mine = excs[g].at[t, k]
        start(g, t, 16, mine.at[pl.ds(5, 11)], mine.at[pl.ds(5, 11)], other)

    def prepare():
        for load in loads[4:7]:
            load.wait()
        mine = cap_ref[:, pl.ds(pl.multiple_of(k * half, half), half)]
        for w in range(weeks):
            cap_rows[w * scens:(w + 1) * scens, :] = jnp.broadcast_to(
                mine[w:w + 1, :], (scens, half)
            )
        for load in loads[7:]:
            load.wait()
        risk = risk_ref[...]
        fail = fw_ref[...]
        for w in range(weeks):
            spacing = (fail - w).astype(F32)
            target = jnp.where(spacing >= 0, 1.0 / (1.0 + (spacing * 0.25) ** 2), 0.25)
            at = slice(w * scens, (w + 1) * scens)
            base[at, :] = STEP * (risk * target - mult[at, :] + plan[at, :])
        have = by_scenario(
            bundle_ref, lax.rem(lax.broadcasted_iota(jnp.int32, (span, 128), 1), scens)
        )
        have = jnp.concatenate([have] * (span // 128), axis=1)
        take = (want == have).astype(F32)
        mixer[...] = jnp.where(r // scens == c // scens, take, 0.0).astype(BF16)
        likes[...] = by_scenario(like_ref, lax.broadcasted_iota(jnp.int32, (scens, cols), 0))

    head, tail = bundle_ref[0], bundle_ref[scens - 1]
    moving = {}

    def edge_start(g, n, source, step):
        at = g * 4 + n
        moving[g, n] = pltpu.make_async_remote_copy(
            src_ref=source, dst_ref=gots[g].at[n], send_sem=edge_send.at[at],
            recv_sem=edge_recv.at[at], device_id=row(step), device_id_type=MESH,
        )
        moving[g, n].start()

    def weeks_of(g):
        lowest = first_of[g] // scens
        return lowest, min(weeks, lowest + chips * rows_of[g] // scens)

    def phase_edges(g, t):
        arrive(g, t - 1, (15, 16))
        update(g, t - 1)
        count = chips * rows_of[g]
        at = slice(first_of[g], first_of[g] + count)
        x = plan[at, :].reshape(count // scens, scens, cols) * likes[...][None]
        high, low = split(x.reshape(count, cols))
        for n, (which, step) in enumerate(((tail, 1), (head, -1))):
            kept = edges[g].shape[1] - (8 if g == 0 else 0)
            week = lax.broadcasted_iota(jnp.int32, (kept, count), 0)
            place = lax.broadcasted_iota(jnp.int32, (kept, count), 1)
            flag = by_scenario(bundle_ref, lax.rem(place, scens)) == which
            take = jnp.where(place // scens == week, flag.astype(F32), 0.0).astype(BF16)
            edges[g][n, 0:kept] = dot(take, high) + dot(take, low)
            if g == 0:
                weight = jnp.float32(0.0)
                for s in range(scens):
                    weight = weight + jnp.where(bundle_ref[s] == which, like_ref[s], 0.0)
                edges[g][n, kept:kept + 8] = jnp.where(
                    lax.broadcasted_iota(jnp.int32, (8, cols), 0) < 4,
                    which.astype(F32), weight,
                )
            edge_start(g, n, edges[g].at[n], step)
            edge_start(g, n + 2, edges[g].at[n], 2 * step)
        for low_row in range(0, count, span):
            size = min(span, count - low_row)
            take = mixer[:size, :size]
            means[first_of[g] + low_row:first_of[g] + low_row + size, :] = (
                dot(take, high[low_row:low_row + size]) + dot(take, low[low_row:low_row + size])
            )
    phases = (phase_core, phase_near, phase_far, phase_back, phase_spread, phase_share)
    steps = [iter([(p, t) for t in range(ITERS) for p in phases] + [(phase_edges, ITERS)])
             for _ in groups]
    for n, g in enumerate(ORDER):
        if n == 2 * len(TILES):
            prepare()
        phase, t = next(steps[g])
        phase(g, t)
    high, low = split(likes[...])
    take = mixer[:scens, :scens]
    weight = dot(take, high) + dot(take, low)
    own = by_scenario(bundle_ref, lax.broadcasted_iota(jnp.int32, (scens, cols), 0))
    at_head, at_tail = (own == head).astype(F32), (own == tail).astype(F32)
    flags, stores = {}, []
    for g in groups:
        lowest, highest = weeks_of(g)
        for n in range(4):
            moving[g, n].wait_recv()
        got = gots[g]
        if g == 0:
            kept = got.shape[1] - 8
            for n in range(4):
                which = tail if n % 2 else head
                flags[n] = (got[n, kept:kept + 1, :] == which.astype(F32)).astype(F32)
                more = flags[n] * got[n, kept + 4:kept + 5, :]
                weight = weight + (at_tail if n % 2 else at_head) * more
            weight = 1.0 / weight
        left = flags[0] * got[0] + flags[2] * got[2]
        right = flags[1] * got[1] + flags[3] * got[3]
        for w in range(lowest, highest):
            at = slice(w * scens, (w + 1) * scens)
            n = w - lowest
            mean = weight * (
                means[at, :] + at_head * left[n:n + 1, :] + at_tail * right[n:n + 1, :]
            )
            means[at, :] = mean
            mult[at, :] = mult[at, :] + (plan[at, :] - mean)
        at = pl.ds(lowest * scens, (highest - lowest) * scens)
        for n, (source, target) in enumerate(((mult, new_ref), (means, bc_ref))):
            stores.append(
                pltpu.make_async_copy(source.at[at], target.at[at], store_sem.at[2 * g + n])
            )
            stores[-1].start()
    for store in stores:
        store.wait()
    for c in (*flying.values(), *moving.values()):
        c.wait_send()


def deliver(a_ref, b_ref, a_out, b_out, room, taken, given):
    pieces = room.shape[1]
    size = room.shape[2]
    ins, outs = [], []
    for n in range(pieces):
        at = pl.ds(n * size, size)
        for m, (source, target) in enumerate(((a_ref, a_out), (b_ref, b_out))):
            ins.append(pltpu.make_async_copy(source.at[at], room.at[m, n], taken.at[m, n]))
            outs.append(pltpu.make_async_copy(room.at[m, n], target.at[at], given.at[m, n]))
    for copy in ins:
        copy.start()
    for copy, onward in zip(ins, outs, strict=True):
        copy.wait()
        onward.start()
    for copy in outs:
        copy.wait()


def local(
    multiplier, consensus_old, failure_week, crew_index, labor_hours, capacity, risk_weight,
    likelihood, bundle_index,
):
    scens, weeks, cols = multiplier.shape
    crews = capacity.shape[0]
    half = crews // 2
    chips = lax.axis_size("comp") // 2
    live = scens * weeks
    padded = chips * 8 * sum(TILES)

    def each(*shape):
        return [pltpu.VMEM(tuple(8 * n if s == "r" else s for s in shape), F32) for n in TILES]

    def edge(count):
        return [
            pltpu.VMEM((count, chips * 8 * n // scens + (8 if g == 0 else 0), cols), F32)
            for g, n in enumerate(TILES)
        ]

    def flat(x):
        return jnp.swapaxes(x, 0, 1).reshape(live, cols)

    hbm = pl.BlockSpec(memory_space=pltpu.HBM)
    copies = len(TILES) * ITERS * NCOPY
    outs = pl.pallas_call(
        kernel,
        out_shape=[jax.ShapeDtypeStruct((live, cols), F32)] * 2,
        in_specs=[hbm] * 9,
        out_specs=[hbm, hbm],
        scratch_shapes=[
            pltpu.VMEM((scens, cols), jnp.int32),
            pltpu.VMEM((1, cols), jnp.int32),
            pltpu.VMEM((1, cols), F32),
            pltpu.VMEM((weeks, crews), F32),
            pltpu.VMEM((1, cols), F32),
            pltpu.SMEM((scens,), F32),
            pltpu.SMEM((scens,), jnp.int32),
            pltpu.VMEM((live, cols), F32),
            pltpu.VMEM((live, cols), F32),
            pltpu.VMEM((padded, cols), F32),
            pltpu.VMEM((padded, cols), F32),
            pltpu.VMEM((crews, cols), BF16),
            pltpu.VMEM((padded, half), F32),
            pltpu.VMEM((256, 256), BF16),
            pltpu.VMEM((scens, cols), F32),
            pltpu.VMEM((padded, cols), F32),
            pltpu.SemaphoreType.DMA((9,)),
            pltpu.SemaphoreType.DMA((2 * len(TILES),)),
            pltpu.SemaphoreType.DMA((copies,)),
            pltpu.SemaphoreType.DMA((copies,)),
            pltpu.SemaphoreType.DMA((4 * len(TILES),)),
            pltpu.SemaphoreType.DMA((4 * len(TILES),)),
            *each(2, chips, "r", half),
            *each(ITERS, chips, "r", half),
            *each(ITERS, 2, 5, "r", half),
            *each(ITERS, "r", half),
            *each(5, "r", half),
            *each(ITERS, 4, "r", half),
            *each(ITERS, 2, chips, "r", half),
            *edge(2),
            *edge(4),
        ],
        compiler_params=pltpu.CompilerParams(
            collective_id=0, has_side_effects=True, vmem_limit_bytes=60 << 20
        ),
        name="hedge",
    )(
        flat(multiplier), flat(consensus_old), failure_week, crew_index.reshape(1, -1),
        labor_hours.reshape(1, -1), capacity.T, risk_weight.reshape(1, -1), likelihood, bundle_index,
    )
    pieces = 4
    outs = pl.pallas_call(
        deliver,
        out_shape=[jax.ShapeDtypeStruct((live, cols), F32)] * 2,
        in_specs=[hbm] * 2,
        out_specs=[hbm] * 2,
        scratch_shapes=[
            pltpu.VMEM((2, pieces, live // pieces, cols), F32),
            pltpu.SemaphoreType.DMA((2, pieces)),
            pltpu.SemaphoreType.DMA((2, pieces)),
        ],
        compiler_params=pltpu.CompilerParams(vmem_limit_bytes=60 << 20),
        name="deliver",
    )(*outs)
    return tuple(jnp.swapaxes(x.reshape(weeks, scens, cols), 0, 1) for x in outs)


def solution(mesh):
    return jax.shard_map(
        local,
        mesh=mesh,
        in_specs=(
            P("scen", None, "comp"),
            P(None, None, "comp"),
            P("scen", "comp"),
            P("comp"),
            P("comp"),
            P(),
            P("comp"),
            P("scen"),
            P("scen"),
        ),
        out_specs=(P("scen", None, "comp"), P("scen", None, "comp")),
        check_vma=False,
    )
```

time: 794 us -> 113 us (0.14)
  waiting for transfers between devices: 707 us -> 0 us
  Pallas kernels: 0 us -> 112 us
  blocking collectives: 33.5 us -> 0 us
  matrix products: 28.6 us -> 0 us
  between operations: 13.9 us -> 0.64 us
    psum x4 -> x0, waiting for transfers between devices: 707 us -> none  [the longest x3 623 us: local(): crew_load = lax.psum(partial_load, 'comp')]
    pallas_call x0 -> x2, Pallas kernels: none -> 112 us  [the longest x1 110 us: local(): pl.pallas_call(kernel, out_shape=[jax.ShapeDtypeStruct((live, cols), F32)...]
    psum x1 -> x0, blocking collectives: 33.5 us -> none  [local(): totals, weight_sum = lax.psum((partial_totals, partial_weights), 'scen')]
    dot_general x9 -> x0, matrix products: 28.6 us -> none  [the longest x3 10.3 us: local(): partial_load = jnp.einsum('swc,ck->swk', plan, labor_hot, precision=highest)]
  transfers between devices with their start and end apart: 4 -> 0, of which waited for: 4 -> 0; matrix products, arithmetic and copies ran while one was open for 0% -> 0% of each run, Pallas kernels for 0% -> 0%
where the time goes in v2:
time: 113 us
  Pallas kernels  112 us (99%)
    pallas_call x1, Pallas kernels, local(): pl.pallas_call(kernel, out_shape=[jax.ShapeDtypeStruct((live, cols), F32)...  110 us
    pallas_call x1, Pallas kernels, local(): pl.pallas_call(deliver, out_shape=[jax.ShapeDtypeStruct((live, cols), F32...  2.89 us

profile of v2, /device:TPU:1, one launch (start us, length us, event | category | flops | bytes accessed | tf_op | source)
XLA Modules:
  0.0 113.1 jit_solution(6489482954180426759)
XLA Ops:
  0.6 109.6 %hedge.1 = (f32[832,512]{1,0:T(8,128)}, f32[832,512]{1,0:T(8,128)}) custom-call(f32[832,512]{1,0:T(8,128)} %bitcast.16, f32[832,512]{1,0:T(8,128)} %bitcast.17, s32[16,512]{1,0:T(8,128)} %fw_hbm.1, s32[1,512]{1,0:T(1,128)} %bitcast.19, f32[1,512]{1,0:T(1,128)} %bitcast.20, f32[52,256]{1,0:T(8,128)} %bitcast.18, f32[1,512]{1,0:T(1,128)} %bitcast.21, ...), custom_call_target="tpu_custom_call" | custom-call | tf_op jit(solution)/shard_map/hedge/pallas_call | solution.py:381
  110.2 2.9 %deliver.1 = (f32[832,512]{1,0:T(8,128)}, f32[832,512]{1,0:T(8,128)}) custom-call(f32[832,512]{1,0:T(8,128)} %get-tuple-element.6.a_ref, f32[832,512]{1,0:T(8,128)} %get-tuple-element.7.b_ref), custom_call_target="tpu_custom_call" | custom-call | tf_op jit(solution)/shard_map/deliver/pallas_call | solution.py:428

commit v3 on v2

--- a/solution.py
+++ b/solution.py
@@ -78,7 +78,7 @@
             (fw_hbm, fw_ref), (mult_hbm, mult),
         ))
     ]
-    for load in loads:
+    for load in loads[:4]:
         load.start()
 
     barrier = pltpu.get_barrier_semaphore()
@@ -112,13 +112,18 @@
     loads[3].wait()
     loads[2].wait()
     labor = labor_ref[...]
-    for at in range(0, live, span):
-        size = min(span, live - at)
-        x = cons[at:at + size, :]
-        high, low = split(x)
-        lower = (x - high.astype(F32) - low.astype(F32)).astype(BF16)
-        take = mixer[:size, :size]
-        plan[at:at + size, :] = dot(take, high) + dot(take, low) + dot(take, lower)
+    for load in loads[4:]:
+        load.start()
+
+    def anchor(g):
+        last = min(live, first_of[g] + chips * rows_of[g])
+        for at in range(first_of[g], last, span):
+            size = min(span, last - at)
+            x = cons[at:at + size, :]
+            high, low = split(x)
+            lower = (x - high.astype(F32) - low.astype(F32)).astype(BF16)
+            take = mixer[:size, :size]
+            plan[at:at + size, :] = dot(take, high) + dot(take, low) + dot(take, lower)
 
     flying = {}
 
@@ -172,6 +177,8 @@
         if t > 0:
             arrive(g, t - 1, (15, 16))
             sent(g, t - 1, (0,))
+        else:
+            anchor(g)
         update(g, t - 1)
         if t == 0 and g == 0:
             pl.semaphore_wait(barrier, len(greeted))

time: 113 us -> 115 us (1.018)
  Pallas kernels: 112 us -> 114 us
    pallas_call x1, Pallas kernels: 110 us -> 111 us  [local(): pl.pallas_call(kernel, out_shape=[jax.ShapeDtypeStruct((live, cols), F32)...]
where the time goes in v3:
time: 115 us; the launch traced here: 114 us
  Pallas kernels  114 us (99%)
    pallas_call x1, Pallas kernels, local(): pl.pallas_call(kernel, out_shape=[jax.ShapeDtypeStruct((live, cols), F32)...  111 us
    pallas_call x1, Pallas kernels, local(): pl.pallas_call(deliver, out_shape=[jax.ShapeDtypeStruct((live, cols), F32...  2.89 us

profile of v3, /device:TPU:1, one launch (start us, length us, event | category | flops | bytes accessed | tf_op | source)
XLA Modules:
  0.0 114.5 jit_solution(11214079987202616027)
XLA Ops:
  0.6 110.9 %hedge.1 = (f32[832,512]{1,0:T(8,128)}, f32[832,512]{1,0:T(8,128)}) custom-call(f32[832,512]{1,0:T(8,128)} %bitcast.16, f32[832,512]{1,0:T(8,128)} %bitcast.17, s32[16,512]{1,0:T(8,128)} %fw_hbm.1, s32[1,512]{1,0:T(1,128)} %bitcast.19, f32[1,512]{1,0:T(1,128)} %bitcast.20, f32[52,256]{1,0:T(8,128)} %bitcast.18, f32[1,512]{1,0:T(1,128)} %bitcast.21, ...), custom_call_target="tpu_custom_call" | custom-call | tf_op jit(solution)/shard_map/hedge/pallas_call | solution.py:388
  111.6 2.9 %deliver.1 = (f32[832,512]{1,0:T(8,128)}, f32[832,512]{1,0:T(8,128)}) custom-call(f32[832,512]{1,0:T(8,128)} %get-tuple-element.6.a_ref, f32[832,512]{1,0:T(8,128)} %get-tuple-element.7.b_ref), custom_call_target="tpu_custom_call" | custom-call | tf_op jit(solution)/shard_map/deliver/pallas_call | solution.py:435
